TPU v7x, 512 devices: a whole 4x4x16 slice. The times are simulated.
512 devices in a mesh: frame: 32 (over z, y_lo), head: 16 (over y_hi, x, core).
Axes of the slice: x: 4, y: 4 (y_hi: 2, y_lo: 2; y = y_hi * 2 + y_lo), z: 16, core: 2. Of those that a mesh axis runs over, the one named last changes fastest.
Arguments:
- latents: bfloat16 [32, 512, 1152], P('frame', 'head'), may hold values from -9 to 9
- spatial_qkv: bfloat16 [3, 1152, 1152], P(None, 'head'), may hold values from -0.5 to 0.5
- spatial_out: bfloat16 [1152, 1152], P('head'), may hold values from -0.375 to 0.375
- temporal_qkv: bfloat16 [3, 1152, 1152], P(None, 'head'), may hold values from -0.5 to 0.5
- temporal_out: bfloat16 [1152, 1152], P('head'), may hold values from -0.375 to 0.375
- modulation: float32 [4, 1152], replicated, may hold values from -2.5 to 2.5
- gates: float32 [2, 1152], replicated, may hold values from 0.5 to 2
- out_bias: float32 [2, 1152], replicated, may hold values from -2.5 to 2.5
Outputs:
- mixed: bfloat16 [32, 512, 1152], P('frame', 'head')
All inputs are finite; a program needn't handle non-finite values.
Results may differ from a plain program's by a relative error of at most 0.015.
Values may be sent and summed in bfloat16 or wider, within the bound.
A program may use at most 64 MiB of HBM per device.

v0:
```python
import jax
import jax.numpy as jnp
from jax import lax
from jax.sharding import PartitionSpec as P

HD = 72


def normalize(tensor, shift_row, scale_row):
    values = tensor.astype(jnp.float32)
    centre = jnp.mean(values, axis=-1, keepdims=True)
    offsets = values - centre
    spread = jnp.mean(offsets * offsets, axis=-1, keepdims=True)
    return (offsets * lax.rsqrt(spread + 1e-06) * (1.0 + scale_row) + shift_row).astype(
        jnp.bfloat16
    )


def project_heads(ready, weight):
    product = lax.dot_general(
        weight, ready, (((2,), (ready.ndim - 1,)), ((), ())), preferred_element_type=jnp.float32
    )
    return product.astype(jnp.bfloat16)


def add_rows(segment, flat_heads):
    return lax.dot_general(
        flat_heads, segment, (((0,), (0,)), ((), ())), preferred_element_type=jnp.float32
    )


def local(
    latents, spatial_qkv, spatial_out, temporal_qkv, temporal_out, modulation, gates, out_bias
):
    frames_dev, local_pos, features = latents.shape
    head_count = lax.axis_size("head")
    frame_count = lax.axis_size("frame")
    channels = spatial_qkv.shape[1]
    heads_dev = channels // HD
    positions = local_pos * head_count
    pair_count = local_pos // frame_count
    frames = frames_dev * frame_count
    inv_root = HD ** (-0.5)
    ready = normalize(
        lax.all_gather(latents, "head", axis=1, tiled=True), modulation[0], modulation[1]
    )
    projected = project_heads(ready, spatial_qkv)
    queries = projected[0].reshape(heads_dev, HD, frames_dev, positions)
    key_rows = projected[1].reshape(heads_dev, HD, frames_dev, positions)
    values = projected[2].reshape(heads_dev, HD, frames_dev, positions)
    block = min(512, positions)
    blocks = positions // block
    query_blocks = jnp.moveaxis(queries.reshape(heads_dev, HD, frames_dev, blocks, block), 3, 0)

    def attend(query_block):
        scores = (
            jnp.einsum("hdfq,hdfk->hfqk", query_block, key_rows, preferred_element_type=jnp.float32)
            * inv_root
        )
        weights = jax.nn.softmax(scores, axis=-1).astype(jnp.bfloat16)
        summed = jnp.einsum("hdfk,hfqk->hdfq", values, weights, preferred_element_type=jnp.float32)
        return summed.astype(jnp.bfloat16)

    attended = lax.map(attend, query_blocks)
    attended = jnp.moveaxis(attended, 0, 3).reshape(channels, frames_dev, positions)
    spatial_tokens = lax.all_to_all(attended, "head", split_axis=2, concat_axis=0, tiled=True)
    spatial_flat = spatial_tokens.reshape(features, frames_dev * local_pos)
    spatial_sum = add_rows(
        lax.all_gather(spatial_out, "head", axis=0, tiled=True), flat_heads=spatial_flat
    )
    spatial_branch = spatial_sum.reshape(frames_dev, local_pos, features) + out_bias[0]
    frame_section = (latents.astype(jnp.float32) + gates[0] * spatial_branch).astype(jnp.bfloat16)
    by_position = lax.all_to_all(frame_section, "frame", split_axis=1, concat_axis=0, tiled=True)
    segment = lax.all_gather(by_position, "head", axis=1, tiled=True)
    ready = normalize(segment, modulation[2], modulation[3])
    product = project_heads(ready, temporal_qkv)
    temporal_all = jnp.swapaxes(product, 2, 3).reshape(3, channels, segment.shape[1] * frames)
    span_count = head_count * pair_count
    t_queries = temporal_all[0].reshape(heads_dev, HD, span_count, frames)
    t_keys = temporal_all[1].reshape(heads_dev, HD, span_count, frames)
    t_values = temporal_all[2].reshape(heads_dev, HD, span_count, frames)
    t_scores = (
        jnp.einsum("hdpq,hdpk->hpqk", t_queries, t_keys, preferred_element_type=jnp.float32)
        * inv_root
    )
    t_weights = jax.nn.softmax(t_scores, axis=-1).astype(jnp.bfloat16)
    t_summed = jnp.einsum(
        "hdpk,hpqk->hdpq", t_values, t_weights, preferred_element_type=jnp.float32
    )
    t_attended = t_summed.astype(jnp.bfloat16).reshape(channels, span_count, frames)
    moved = lax.all_to_all(t_attended, "head", split_axis=1, concat_axis=0, tiled=True)
    temporal_flat = moved.reshape(features, -1)
    temporal_sum = add_rows(
        lax.all_gather(temporal_out, "head", axis=0, tiled=True), flat_heads=temporal_flat
    )
    branch_rows = (
        jnp.swapaxes(temporal_sum.reshape(pair_count, frames, features), 0, 1) + out_bias[1]
    )
    updated = (by_position.astype(jnp.float32) + gates[1] * branch_rows).astype(jnp.bfloat16)
    mixed = lax.all_to_all(updated, "frame", split_axis=0, concat_axis=1, tiled=True)
    return mixed


def solution(mesh):
    return jax.shard_map(
        local,
        mesh=mesh,
        in_specs=(
            P("frame", "head", None),
            P(None, "head", None),
            P("head", None),
            P(None, "head", None),
            P("head", None),
            P(),
            P(),
            P(),
        ),
        out_specs=P("frame", "head", None),
        check_vma=False,
    )
```

profile of v0, /device:TPU:1, one launch (start us, length us, event | category | flops | bytes accessed | tf_op | source)
XLA Modules:
  0.0 337.9 jit_solution(18133003216958481031)
XLA Ops:
  6.5 0.7 all-gather.6.cloned.1.call-update
  7.3 0.7 all-gather.8.cloned.1.call-update
  8.0 0.9 add_reduce_fusion
  8.9 68.4 %all-gather.6.cloned.1.call-done = bf16[1,512,1152]{2,1,0:T(8,128)(2,1)} async-done(((bf16[1,32,1152]{2,1,0:T(8,128)(2,1)}), bf16[1,512,1152]{2,1,0:T(8,128)(2,1)}) %all-gather.6.cloned.1.call-update) | async-done | bytes 1179664 | tf_op jit(solution)/shard_map/all_gather | solution.py:45
  77.3 1.6 convert_reduce_fusion
  78.9 1.7 fusion.3
  80.7 0.8 fusion.30
  81.5 0.4 fusion.47
  81.9 0.2 fusion.35
  82.1 0.3 fusion.34
  82.4 0.2 copy.30
  82.6 0.5 broadcast.106
  83.1 1.5 reduce.28
  84.6 0.9 reshape.199
  85.4 3.9 %all-to-all-start = ((bf16[16,2,1152]{2,1,0:T(2,128)(2,1)}), bf16[16,2,1152]{2,1,0:T(2,128)(2,1)S(1)}, u32[]{:S(2)}, u32[]{:S(2)}) async-start(bf16[16,2,1152]{2,1,0:T(2,128)(2,1)} %reshape.199), calls=%async_computation | async-start | bytes 147456 | tf_op jit(solution)/shard_map/all_to_all | solution.py:66
  89.5 7.2 %all-to-all-done = bf16[16,2,1152]{2,1,0:T(2,128)(2,1)S(1)} async-done(((bf16[16,2,1152]{2,1,0:T(2,128)(2,1)}), bf16[16,2,1152]{2,1,0:T(2,128)(2,1)S(1)}, u32[]{:S(2)}, u32[]{:S(2)}) %all-to-all-start) | async-done | bytes 73760 | tf_op jit(solution)/shard_map/all_to_all | solution.py:66
  96.7 0.5 reshape.200
  97.2 0.1 copy.31
  97.2 0.2 reshape.178
  97.4 48.1 %all-gather.8.cloned.1.call-done = bf16[1152,1152]{1,0:T(8,128)(2,1)} async-done(((bf16[72,1152]{1,0:T(8,128)(2,1)}), bf16[1152,1152]{1,0:T(8,128)(2,1)}) %all-gather.8.cloned.1.call-update) | async-done | bytes 2654224 | tf_op jit(solution)/shard_map/all_gather | solution.py:69
  145.5 2.3 fusion.12
  147.8 0.1 copy.63
  148.0 1.0 reduce.29
  149.0 0.1 reshape.201
  149.1 25.2 %all_to_all.54 = bf16[32,2,576]{2,1,0:T(2,128)(2,1)S(1)} all-to-all(bf16[32,2,576]{2,1,0:T(2,128)(2,1)S(1)} %reshape.201), channel_id=1, replica_groups=mesh['frame'=32,'head'=16] {'frame'}, dimensions={0} | all-to-all | bytes 147456 | tf_op jit(solution)/shard_map/all_to_all | solution.py:73
  174.3 0.8 reshape.202
  175.2 0.2 all-gather.10.cloned.1.call-start
  175.4 0.3 all-gather.10.cloned.1.call-update
  175.8 58.4 %all-gather.12.cloned.1.call-done = bf16[1,32,18432]{2,0,1:T(2,128)(2,1)} async-done(((bf16[1,32,1152]{2,0,1:T(2,128)(2,1)}), bf16[1,32,18432]{2,0,1:T(2,128)(2,1)}) %all-gather.12.cloned.1.call-update) | async-done | bytes 1179664 | tf_op jit(solution)/shard_map/all_gather | solution.py:74
  234.2 8.5 %convert_reduce_fusion.1 = f32[32,18432]{1,0:T(8,128)S(1)} fusion(bf16[1,32,18432]{2,0,1:T(2,128)(2,1)} %all-gather.12.cloned.1.call-done), kind=kLoop, calls=%fused_computation.9 | loop fusion | flops 589824 | bytes 3538944 | tf_op jit(solution)/shard_map/convert_element_type | solution.py:10
  242.7 0.4 copy.44
  243.1 0.2 reduce_sum.58
  243.3 0.4 multiply_reduce_fusion
  243.7 0.4 copy-done.6
  244.1 0.9 fusion.16
  245.1 0.2 fusion.48
  245.3 0.2 convolution_multiply_fusion.1
  245.5 0.3 fusion.33
  245.8 11.3 %all_to_all.55 = bf16[72,16,32]{0,2,1:T(8,128)(2,1)S(1)} all-to-all(bf16[72,16,32]{0,2,1:T(8,128)(2,1)S(1)} %fusion.33), channel_id=1, replica_groups=mesh['frame'=32,'head'=16] {'head'}, dimensions={1} | all-to-all | bytes 147456 | tf_op jit(solution)/shard_map/all_to_all | solution.py:91
  257.1 0.1 copy.38
  257.2 0.2 reshape.183
  257.3 44.9 %all-gather.10.cloned.1.call-done = bf16[1152,1152]{1,0:T(8,128)(2,1)} async-done(((bf16[72,1152]{1,0:T(8,128)(2,1)}), bf16[1152,1152]{1,0:T(8,128)(2,1)}) %all-gather.10.cloned.1.call-update) | async-done | bytes 2654224 | tf_op jit(solution)/shard_map/all_gather | solution.py:94
  302.2 2.3 fusion.14
  304.5 0.6 reduce.30
  305.2 0.1 reshape.203
  305.3 25.2 %all_to_all.56 = bf16[32,2,576]{2,1,0:T(2,128)(2,1)S(1)} all-to-all(bf16[32,2,576]{2,1,0:T(2,128)(2,1)S(1)} %reshape.203), channel_id=1, replica_groups=mesh['frame'=32,'head'=16] {'frame'}, dimensions={0} | all-to-all | bytes 147456 | tf_op jit(solution)/shard_map/all_to_all | solution.py:100
  330.5 0.1 reshape.204
  330.7 0.6 copy.62
  (24 shorter events, 0.3 us)
Async XLA Ops:
  6.5 74.1 %copy-start = (bf16[3,72,1152]{2,1,0:T(8,128)(2,1)S(1)}, bf16[3,72,1152]{2,1,0:T(8,128)(2,1)}, u32[]{:S(2)}) copy-start(bf16[3,72,1152]{2,1,0:T(8,128)(2,1)} %param.9) | copy-start | bytes 1492996
  6.5 70.8 %all-gather.6.cloned.1.call-start = ((), (), s32[]{:S(2)}) async-start(), calls=%async_computation.4 | async-start | bytes 1253376 | tf_op jit(solution)/shard_map/all_gather | solution.py:45
  7.3 138.3 %all-gather.8.cloned.1.call-start = ((), (), s32[]{:S(2)}) async-start(), calls=%async_computation.5 | async-start | bytes 2820096 | tf_op jit(solution)/shard_map/all_gather | solution.py:69
  77.3 3.3 copy-start.1
  82.0 7.3 %copy-start.4 = (f32[2,1152]{1,0:T(2,128)S(1)}, f32[2,1152]{1,0:T(2,128)}, u32[]{:S(2)}) copy-start(f32[2,1152]{1,0:T(2,128)} %param.15) | copy-start | bytes 27652
  82.1 7.3 %copy-start.5 = (f32[2,1152]{1,0:T(2,128)S(1)}, f32[2,1152]{1,0:T(2,128)}, u32[]{:S(2)}) copy-start(f32[2,1152]{1,0:T(2,128)} %param.14) | copy-start | bytes 27652
  82.1 63.4 %copy-start.3 = (bf16[1,32,1152]{2,1,0:T(8,128)(2,1)S(1)}, bf16[1,32,1152]{2,1,0:T(8,128)(2,1)}, u32[]{:S(2)}) copy-start(bf16[1,32,1152]{2,1,0:T(8,128)(2,1)} %param.8) | copy-start | bytes 221188
  85.4 11.3 %all-to-all-start = ((bf16[16,2,1152]{2,1,0:T(2,128)(2,1)}), bf16[16,2,1152]{2,1,0:T(2,128)(2,1)S(1)}, u32[]{:S(2)}, u32[]{:S(2)}) async-start(bf16[16,2,1152]{2,1,0:T(2,128)(2,1)} %reshape.199), calls=%async_computation | async-start | bytes 147456 | tf_op jit(solution)/shard_map/all_to_all | solution.py:66
  89.3 144.9 %all-gather.12.cloned.1.call-start = ((), (), s32[]{:S(2)}) async-start(), calls=%async_computation.7 | async-start | bytes 2506752 | tf_op jit(solution)/shard_map/all_gather | solution.py:74
  175.2 127.0 %all-gather.10.cloned.1.call-start = ((), (), s32[]{:S(2)}) async-start(), calls=%async_computation.6 | async-start | bytes 2820096 | tf_op jit(solution)/shard_map/all_gather | solution.py:94
  243.1 1.0 copy-start.6
  245.1 57.2 %copy-start.2 = (bf16[32,1,1152]{2,1,0:T(2,128)(2,1)S(1)}, bf16[32,1,1152]{2,1,0:T(2,128)(2,1)}, u32[]{:S(2)}) copy-start(bf16[32,1,1152]{2,1,0:T(2,128)(2,1)} %reshape.202) | copy-start | bytes 221188
Sparse Core Ops, SparseCore 0:
  10.7 66.6 all-gather.5
  80.7 64.8 all-gather.7
  175.3 58.8 all-gather.11
  237.4 64.7 all-gather.9
where the time goes:
time: 339 us; the launch traced here: 338 us
  waiting for transfers between devices  229 us (68%)
  blocking collectives  61.7 us (18%)
  other arithmetic  16.6 us (5%)
  between operations  13.4 us (4%)
  matrix products  7.69 us (2%)
  local copies, waits for them, and re-layouts  5.49 us (2%)
  starting transfers between devices  4.22 us (1%)
    all_gather x1, waiting for transfers between devices, local(): lax.all_gather(latents, 'head', axis=1, tiled=True)  68.4 us
    all_gather x1, waiting for transfers between devices, local(): segment = lax.all_gather(by_position, 'head', axis=1, tiled=True)  58.4 us
    all_gather x1, waiting for transfers between devices, local(): lax.all_gather(spatial_out, 'head', axis=0, tiled=True)  48.1 us
    all_gather x1, waiting for transfers between devices, local(): lax.all_gather(temporal_out, 'head', axis=0, tiled=True)  44.9 us
    all_to_all x1, blocking collectives, local(): lax.all_to_all(frame_section, 'frame', split_axis=1, concat_axis=0, tiled...  25.2 us
    all_to_all x1, blocking collectives, local(): lax.all_to_all(updated, 'frame', split_axis=0, concat_axis=1, tiled=True)  25.2 us
    all_to_all x1, blocking collectives, local(): lax.all_to_all(t_attended, 'head', split_axis=1, concat_axis=0, tiled=True)  11.3 us
    convert_element_type x1, other arithmetic, normalize(): values = tensor.astype(jnp.float32)  8.49 us
  transfers between devices with their start and end apart: 5, of which 5 were waited for; matrix products, arithmetic and copies ran while one was open for 6% of the time, Pallas kernels for 0%

commit v1 on v0

v1 whole, which is shorter than its diff:
```python
import functools

import jax
import jax.numpy as jnp
from jax import lax
from jax.experimental import pallas as pl
from jax.experimental.pallas import tpu as pltpu
from jax.sharding import PartitionSpec as P

HD = 72
PAD = 128
WROWS = 80
D = 1152
TOK = 32
HEADS = 16
SCALE2 = HD**-0.5 * 1.4426950408889634
MESH = pl.DeviceIdType.MESH


def normalize(values, shift_row, scale_row):
    centre = jnp.mean(values, axis=-1, keepdims=True)
    offsets = values - centre
    spread = jnp.mean(offsets * offsets, axis=-1, keepdims=True)
    return (offsets * lax.rsqrt(spread + 1e-6) * (1.0 + scale_row) + shift_row).astype(jnp.bfloat16)


def places():
    frame, head = lax.axis_index("frame"), lax.axis_index("head")
    return frame // 2, frame % 2, head // 8, (head // 2) % 4, head % 2


def group_place(half):
    z, yl, yh, x, c = places()
    zg = c * 8 + half * 4 + x
    delta = (z - zg + 16) % 16
    line = ((1 - yl) * delta + yl * (16 - delta)) % 8
    core = (yl + zg // 8 + 1) % 2
    return (zg * 2 + yh, (line // 4) * 8 + (line % 4) * 2 + core), delta // 8


def frame_place(slot):
    z, yl, yh, x, c = places()
    ylf = (c + z // 8 + 1) % 2
    line = yh * 4 + x
    delta = ((1 - ylf) * line + ylf * (8 - line)) % 8 + 8 * slot
    zf = (z + delta) % 16
    return (zf * 2 + ylf, yl * 8 + (z % 4) * 2 + z // 8), (z // 4) % 2


def remote(src, dst, send, recv, device):
    return pltpu.make_async_remote_copy(
        src_ref=src, dst_ref=dst, send_sem=send, recv_sem=recv, device_id=device, device_id_type=MESH
    )


def kernel(
    lat_ref, sqkv_ref, so_ref, tqkv_ref, to_ref, mod_ref, gate_ref, bias_ref,
    out_ref,
    x0, x1, wm0, wm1, wb0, wb1, o0, o1, h0, h1, y0, y1, p0, p1,
    ag_s, ag_r, sib_s, sib_r, w_s, w_r, ws_s, ws_r, a_s, a_r, p_s, p_r,
):
    frame, head = lax.axis_index("frame"), lax.axis_index("head")
    _, _, yh, x, c = places()
    sibling = (frame, yh * 8 + x * 2 + 1 - c)
    pending = []

    def chip(k, sign):
        return ((yh + k // 4) % 2) * 8 + ((x + sign * (k % 4) + 4) % 4) * 2 + c

    barrier = pltpu.get_barrier_semaphore()
    for d in range(1, HEADS):
        pl.semaphore_signal(barrier, inc=1, device_id=(frame, (head + d) % HEADS), device_id_type=MESH)
    for i in range(2):
        pl.semaphore_signal(barrier, inc=1, device_id=group_place(i)[0], device_id_type=MESH)
        pl.semaphore_signal(barrier, inc=1, device_id=frame_place(i)[0], device_id_type=MESH)

    own_rows = pl.ds(pl.multiple_of(head * TOK, TOK), TOK)
    own_w = pl.ds(pl.multiple_of(head * PAD, PAD), WROWS)
    latents = lat_ref[0].astype(jnp.float32)
    x0[own_rows, :] = normalize(latents, mod_ref[0:1, :], mod_ref[1:2, :])
    for wm, qkv_ref in ((wm0, sqkv_ref), (wm1, tqkv_ref)):
        for m in range(3):
            wm[m * PAD + 64 : (m + 1) * PAD, :] = jnp.zeros((64, D), jnp.bfloat16)
            wm[m * PAD : m * PAD + HD, :] = qkv_ref[m]
    for wb, wo_ref in ((wb0, so_ref), (wb1, to_ref)):
        for k in range(HEADS):
            wb[k * PAD + WROWS : (k + 1) * PAD, :] = jnp.zeros((PAD - WROWS, D), jnp.bfloat16)
        wb[own_w, :] = jnp.concatenate([wo_ref[...], jnp.zeros((WROWS - HD, D), jnp.bfloat16)], axis=0)
    pl.semaphore_wait(barrier, HEADS - 1 + 4)

    ORDER = (2, 6, 5, 7, 4, 1, 3)

    def start(copy):
        copy.start()
        pending.append(copy)

    def send_tokens(st, xb):
        start(remote(xb.at[own_rows], xb.at[own_rows], sib_s.at[st, 0], sib_r.at[st, 0], sibling))
        for k in ORDER:
            start(remote(xb.at[own_rows], xb.at[own_rows], ag_s.at[st, k], ag_r.at[st, k], (frame, chip(k, 1))))

    def gather_tokens(st, xb):
        for k in ORDER[::-1]:
            rows = pl.ds(pl.multiple_of(chip(k, -1) * TOK, TOK), TOK)
            remote(xb.at[rows], xb.at[rows], ag_s.at[st, k], ag_r.at[st, k], sibling).wait_recv()
            start(remote(xb.at[rows], xb.at[rows], sib_s.at[st, k], sib_r.at[st, k], sibling))
        for k in (0,) + ORDER[::-1]:
            rows = pl.ds(pl.multiple_of((chip(k, -1) + 1 - 2 * c) * TOK, TOK), TOK)
            remote(xb.at[rows], xb.at[rows], sib_s.at[st, k], sib_r.at[st, k], sibling).wait_recv()

    def send_weight(st, wb):
        start(remote(wb.at[own_w], wb.at[own_w], ws_s.at[st, 0], ws_r.at[st, 0], sibling))
        for k in ORDER:
            start(remote(wb.at[own_w], wb.at[own_w], w_s.at[st, k], w_r.at[st, k], (frame, chip(k, 1))))

    def forward_weight(st, wb):
        for k in ORDER[::-1]:
            rows = pl.ds(pl.multiple_of(chip(k, -1) * PAD, PAD), WROWS)
            remote(wb.at[rows], wb.at[rows], w_s.at[st, k], w_r.at[st, k], sibling).wait_recv()
            start(remote(wb.at[rows], wb.at[rows], ws_s.at[st, k], ws_r.at[st, k], sibling))

    def wait_weight(st, wb):
        for k in (0,) + ORDER[::-1]:
            rows = pl.ds(pl.multiple_of((chip(k, -1) + 1 - 2 * c) * PAD, PAD), WROWS)
            remote(wb.at[rows], wb.at[rows], ws_s.at[st, k], ws_r.at[st, k], sibling).wait_recv()

    def attend(xb, wm, ob, same_position):
        proj = lax.dot_general(
            xb[...], wm[...], (((1,), (1,)), ((), ())), preferred_element_type=jnp.float32
        )
        total = HEADS * TOK
        queries = proj[:, :PAD].astype(jnp.bfloat16)
        keys = proj[:, PAD : 2 * PAD].astype(jnp.bfloat16)
        lane = lax.broadcasted_iota(jnp.int32, (total, PAD), 1)
        values = jnp.where(lane == HD, 1.0, proj[:, 2 * PAD :]).astype(jnp.bfloat16)
        block = 128
        for i in range(total // block):
            scores = lax.dot_general(
                queries[i * block : (i + 1) * block], keys, (((1,), (1,)), ((), ())),
                preferred_element_type=jnp.float32,
            )
            if same_position:
                row = lax.broadcasted_iota(jnp.int32, (block, total), 0)
                col = lax.broadcasted_iota(jnp.int32, (block, total), 1)
                scores = jnp.where(((row - col) & 15) == 0, scores, -1e30)
            largest = jnp.max(scores, axis=-1, keepdims=True)
            weights = jnp.exp2((scores - largest) * SCALE2).astype(jnp.bfloat16)
            summed = jnp.dot(weights, values, preferred_element_type=jnp.float32)
            ob[i * block : (i + 1) * block, :] = (summed / summed[:, HD : HD + 1]).astype(jnp.bfloat16)

    def send_heads(st, ob, hb):
        hb[pl.ds(head, 1)] = ob[own_rows, :].reshape(1, TOK, PAD)
        for d in range(1, HEADS):
            other = (head + d) % HEADS
            rows = pl.ds(pl.multiple_of(other * TOK, TOK), TOK)
            start(remote(ob.at[rows], hb.at[head], a_s.at[st, d], a_r.at[st, d], (frame, other)))

    def project(st, hb, wb):
        for d in range(1, HEADS):
            other = (head + HEADS - d) % HEADS
            remote(hb.at[other], hb.at[other], a_s.at[st, d], a_r.at[st, d], sibling).wait_recv()
        flat = jnp.concatenate([hb[k] for k in range(HEADS)], axis=1)
        branch = jnp.dot(flat, wb[...], preferred_element_type=jnp.float32)
        return gate_ref[st : st + 1, :] * (branch + bias_ref[st : st + 1, :])

    send_tokens(0, x0)
    gather_tokens(0, x0)
    send_weight(0, wb0)
    attend(x0, wm0, o0, False)
    send_heads(0, o0, h0)
    forward_weight(0, wb0)
    wait_weight(0, wb0)
    y0[...] = (latents + project(0, h0, wb0)).astype(jnp.bfloat16)

    for i in range(2):
        device, slot = group_place(i)
        start(remote(y0.at[i * 16 : i * 16 + 16], p0.at[slot], p_s.at[0, i], p_r.at[0, slot], device))
    send_weight(1, wb1)
    for i in range(2):
        remote(p0.at[i], p0.at[i], p_s.at[0, i], p_r.at[0, i], sibling).wait_recv()

    section = p0[...].reshape(TOK, D).astype(jnp.float32)
    x1[own_rows, :] = normalize(section, mod_ref[2:3, :], mod_ref[3:4, :])
    send_tokens(1, x1)
    gather_tokens(1, x1)
    attend(x1, wm1, o1, True)
    send_heads(1, o1, h1)
    forward_weight(1, wb1)
    wait_weight(1, wb1)
    y1[...] = (section + project(1, h1, wb1)).astype(jnp.bfloat16)

    for i in range(2):
        device, half = frame_place(i)
        start(remote(y1.at[i * 16 : i * 16 + 16], p1.at[half], p_s.at[1, i], p_r.at[1, half], device))
    for i in range(2):
        remote(p1.at[i], p1.at[i], p_s.at[1, i], p_r.at[1, i], sibling).wait_recv()
    out_ref[...] = p1[...].reshape(1, TOK, D)
    for copy in pending:
        copy.wait_send()


def local(latents, spatial_qkv, spatial_out, temporal_qkv, temporal_out, modulation, gates, out_bias):
    bf16, vmem, dma = jnp.bfloat16, pltpu.VMEM, pltpu.SemaphoreType.DMA
    total = HEADS * TOK
    return pl.pallas_call(
        kernel,
        out_shape=jax.ShapeDtypeStruct(latents.shape, bf16),
        in_specs=[pl.BlockSpec(memory_space=pltpu.VMEM)] * 8,
        out_specs=pl.BlockSpec(memory_space=pltpu.VMEM),
        scratch_shapes=[
            vmem((total, D), bf16), vmem((total, D), bf16),
            vmem((3 * PAD, D), bf16), vmem((3 * PAD, D), bf16),
            vmem((HEADS * PAD, D), bf16), vmem((HEADS * PAD, D), bf16),
            vmem((total, PAD), bf16), vmem((total, PAD), bf16),
            vmem((HEADS, TOK, PAD), bf16), vmem((HEADS, TOK, PAD), bf16),
            vmem((TOK, D), bf16), vmem((TOK, D), bf16),
            vmem((2, TOK // 2, D), bf16), vmem((2, TOK // 2, D), bf16),
            dma((2, 8)), dma((2, 8)), dma((2, 8)), dma((2, 8)),
            dma((2, 8)), dma((2, 8)), dma((2, 8)), dma((2, 8)),
            dma((2, 16)), dma((2, 16)), dma((2, 2)), dma((2, 2)),
        ],
        compiler_params=pltpu.CompilerParams(
            collective_id=0, has_side_effects=True, vmem_limit_bytes=48 << 20
        ),
        name="block_pair",
    )(latents, spatial_qkv, spatial_out, temporal_qkv, temporal_out, modulation, gates, out_bias)


def solution(mesh):
    return jax.shard_map(
        local,
        mesh=mesh,
        in_specs=(
            P("frame", "head", None),
            P(None, "head", None),
            P("head", None),
            P(None, "head", None),
            P("head", None),
            P(),
            P(),
            P(),
        ),
        out_specs=P("frame", "head", None),
        check_vma=False,
    )
```

time: 339 us -> 108 us (0.32)
  waiting for transfers between devices: 229 us -> 0 us
  Pallas kernels: 0 us -> 99.7 us
  blocking collectives: 61.7 us -> 0 us
  other arithmetic: 16.6 us -> 0 us
  between operations: 13.4 us -> 0.02 us
  matrix products: 7.69 us -> 0 us
  starting transfers between devices: 4.22 us -> 0 us
    all_gather x4 -> x0, waiting for transfers between devices: 220 us -> none  [the longest x1 68.4 us: local(): lax.all_gather(latents, 'head', axis=1, tiled=True)]
    pallas_call x0 -> x1, Pallas kernels: none -> 99.7 us  [local(): pl.pallas_call(kernel, out_shape=jax.ShapeDtypeStruct(latents.shape, bf16...]
    all_to_all x3 -> x0, blocking collectives: 61.7 us -> none  [the longest x1 25.2 us: local(): lax.all_to_all(frame_section, 'frame', split_axis=1, concat_axis=0, tiled...]
    convert_element_type x2 -> x0, other arithmetic: 9.12 us -> none  [the longest x1 8.49 us: normalize(): values = tensor.astype(jnp.float32)]
    dot_general x8 -> x0, matrix products: 7.45 us -> none  [the longest x2 4.64 us: add_rows(): lax.dot_general(flat_heads, segment, (((0,), (0,)), ((), ())), preferred_...]
    all_to_all x1 -> x0, waiting for transfers between devices: 7.21 us -> none  [local(): lax.all_to_all(attended, 'head', split_axis=2, concat_axis=0, tiled=True)]
    reduce_sum x5 -> x0, other arithmetic: 4.06 us -> none  [the longest x2 2.08 us: normalize(): spread = jnp.mean(offsets * offsets, axis=-1, keepdims=True)]
    all_to_all x1 -> x0, starting transfers between devices: 3.92 us -> none  [local(): lax.all_to_all(attended, 'head', split_axis=2, concat_axis=0, tiled=True)]
  transfers between devices with their start and end apart: 5 -> 0, of which waited for: 5 -> 0; matrix products, arithmetic and copies ran while one was open for 6% -> 0% of each run, Pallas kernels for 0% -> 0%
where the time goes in v1:
time: 108 us; the launch traced here: 107 us
  Pallas kernels  99.7 us (92%)
  local copies, waits for them, and re-layouts  7.53 us (7%)
    pallas_call x1, Pallas kernels, local(): pl.pallas_call(kernel, out_shape=jax.ShapeDtypeStruct(latents.shape, bf16...  99.7 us
    unnamed x17, local copies, waits for them, and re-layouts  7.53 us

profile of v1, /device:TPU:1, one launch (start us, length us, event | category | flops | bytes accessed | tf_op | source)
XLA Modules:
  0.0 107.3 jit_solution(13786434086068598058)
XLA Ops:
  0.0 0.0 copy-start
  0.0 1.0 copy-done
  1.0 0.0 copy-start.1
  1.0 1.0 copy-done.1
  2.1 0.0 copy-start.2
  2.1 0.9 copy-done.2
  3.0 0.0 copy-start.3
  3.0 0.9 copy-done.3
  3.9 0.0 copy-start.4
  3.9 0.9 copy-done.4
  4.8 0.0 copy-start.5
  4.8 0.7 copy-done.5
  5.5 0.0 copy-start.6
  5.5 0.7 copy-done.6
  6.2 0.0 copy-start.7
  6.2 0.7 copy-done.7
  6.9 99.7 %block_pair.1 = bf16[1,32,1152]{2,1,0:T(8,128)(2,1)S(1)} custom-call(bf16[1,32,1152]{2,1,0:T(8,128)(2,1)S(1)} %copy-done.4, bf16[3,72,1152]{2,1,0:T(8,128)(2,1)S(1)} %copy-done, bf16[72,1152]{1,0:T(8,128)(2,1)S(1)} %copy-done.2, bf16[3,72,1152]{2,1,0:T(8,128)(2,1)S(1)} %copy-done.1, bf16[72,1152]{1,0:T(8,128)(2,1)S(1)} %copy-done.3, ...), custom_call_target="tpu_custom_call" | custom-call | tf_op jit(solution)/shard_map/block_pair/pallas_call | solution.py:205
  106.7 0.6 copy.10
Async XLA Ops:
  0.0 1.0 copy-start
  1.0 1.0 copy-start.1
  2.1 0.9 copy-start.2
  3.0 0.9 copy-start.3
  3.9 0.9 copy-start.4
  4.8 0.7 copy-start.5
  5.5 0.7 copy-start.6
  6.2 0.7 copy-start.7

commit v2 on v1

v2 whole, which is shorter than its diff:
```python
import jax
import jax.numpy as jnp
from jax import lax
from jax.experimental import pallas as pl
from jax.experimental.pallas import tpu as pltpu
from jax.sharding import PartitionSpec as P

HD = 72
PAD = 128
D = 1152
TOK = 32
TOTAL = 512
NEAR = (1, 3, 4, 2, 5, 7, 6)
FAR = NEAR[::-1]
SCALE2 = HD**-0.5 * 1.4426950408889634
MESH = pl.DeviceIdType.MESH


def normalize(values, shift_row, scale_row):
    centre = jnp.mean(values, axis=-1, keepdims=True)
    offsets = values - centre
    spread = jnp.mean(offsets * offsets, axis=-1, keepdims=True)
    return (offsets * lax.rsqrt(spread + 1e-6) * (1.0 + scale_row) + shift_row).astype(jnp.bfloat16)


def places():
    frame, head = lax.axis_index("frame"), lax.axis_index("head")
    return frame // 2, frame % 2, head // 8, (head // 2) % 4, head % 2


def group_place(half):
    z, yl, yh, x, c = places()
    zg = c * 8 + half * 4 + x
    delta = (z - zg + 16) % 16
    line = ((1 - yl) * delta + yl * (16 - delta)) % 8
    core = (yl + zg // 8 + 1) % 2
    return (zg * 2 + yh, (line // 4) * 8 + (line % 4) * 2 + core), delta // 8


def frame_place(slot):
    z, yl, yh, x, c = places()
    ylf = (c + z // 8 + 1) % 2
    line = yh * 4 + x
    delta = ((1 - ylf) * line + ylf * (8 - line)) % 8 + 8 * slot
    zf = (z + delta) % 16
    return (zf * 2 + ylf, yl * 8 + (z % 4) * 2 + z // 8), (z // 4) % 2


def remote(src, dst, send, recv, device):
    return pltpu.make_async_remote_copy(
        src_ref=src, dst_ref=dst, send_sem=send, recv_sem=recv, device_id=device, device_id_type=MESH
    )


def kernel(
    lat_hbm, sqkv_hbm, so_hbm, tqkv_hbm, to_hbm, mod_hbm, gate_hbm, bias_hbm,
    out_ref,
    lat_ref, qkv0, qkv1, wo0, wo1, mod_ref, gate_ref, bias_ref,
    x0, x1, wm0, wm1, wp0, wp1, o0, o1, u0, u1, v0, v1, t0, t1, r0, r1, acc, y0, y1, p0, p1,
    in_s, ag_s, ag_r, sib_s, sib_r, u_s, u_r, t_s, t_r, p_s, p_r,
):
    frame = lax.axis_index("frame")
    z, yl, yh, x, c = places()
    head = yh * 8 + x * 2 + c
    sibling = (frame, yh * 8 + x * 2 + 1 - c)
    pending = []

    def chip(k, sign):
        return ((yh + k // 4) % 2) * 4 + (x + sign * (k % 4) + 4) % 4

    def start(copy):
        copy.start()
        pending.append(copy)

    barrier = pltpu.get_barrier_semaphore()
    for i in range(2):
        pl.semaphore_signal(barrier, inc=1, device_id=group_place(i)[0], device_id_type=MESH)
        pl.semaphore_signal(barrier, inc=1, device_id=frame_place(i)[0], device_id_type=MESH)
    for k in NEAR[::-1]:
        pl.semaphore_signal(barrier, inc=1, device_id=(frame, chip(k, 1) * 2 + c), device_id_type=MESH)
    pl.semaphore_signal(barrier, inc=1, device_id=sibling, device_id_type=MESH)

    loads = [
        pltpu.make_async_copy(src, dst, in_s.at[i])
        for i, (src, dst) in enumerate((
            (lat_hbm, lat_ref), (mod_hbm, mod_ref), (sqkv_hbm, qkv0), (so_hbm, wo0), (gate_hbm, gate_ref),
            (bias_hbm, bias_ref), (tqkv_hbm, qkv1), (to_hbm, wo1),
        ))
    ]
    for load in loads:
        load.start()

    def own_rows(core):
        return pl.ds(pl.multiple_of((yh * 4 + x) * 64 + core * TOK, TOK), TOK)

    def rows_of(k, sign, core):
        return pl.ds(pl.multiple_of(chip(k, sign) * 64 + core * TOK, TOK), TOK)

    def send_tokens(st, xb):
        rows = own_rows(c)
        for k in NEAR:
            start(remote(xb.at[rows], xb.at[rows], ag_s.at[st, k], ag_r.at[st, k], (frame, chip(k, 1) * 2 + c)))
        start(remote(xb.at[rows], xb.at[rows], sib_s.at[st, 0], sib_r.at[st, 0], sibling))

    def gather_tokens(st, xb):
        for k in NEAR:
            rows = rows_of(k, -1, c)
            remote(xb.at[rows], xb.at[rows], ag_s.at[st, k], ag_r.at[st, k], sibling).wait_recv()
            start(remote(xb.at[rows], xb.at[rows], sib_s.at[st, k], sib_r.at[st, k], sibling))
        for k in (0,) + NEAR:
            rows = rows_of(k, -1, 1 - c)
            remote(xb.at[rows], xb.at[rows], sib_s.at[st, k], sib_r.at[st, k], sibling).wait_recv()

    def prepare(wm, qkv_ref, wp, wo_ref):
        for m in range(3):
            wm[m * PAD + 64 : (m + 1) * PAD, :] = jnp.zeros((64, D), jnp.bfloat16)
            wm[m * PAD : m * PAD + HD, :] = qkv_ref[m]
        wp[64:, :] = jnp.zeros((64, D), jnp.bfloat16)
        wp[:HD, :] = wo_ref[...]

    def attend(xb, wm, ob, same_position):
        proj = lax.dot_general(
            xb[...], wm[...], (((1,), (1,)), ((), ())), preferred_element_type=jnp.float32
        )
        queries = proj[:, :PAD].astype(jnp.bfloat16)
        keys = proj[:, PAD : 2 * PAD].astype(jnp.bfloat16)
        lane = lax.broadcasted_iota(jnp.int32, (TOTAL, PAD), 1)
        values = jnp.where(lane == HD, 1.0, proj[:, 2 * PAD :]).astype(jnp.bfloat16)
        block = 128
        for i in range(TOTAL // block):
            scores = lax.dot_general(
                queries[i * block : (i + 1) * block], keys, (((1,), (1,)), ((), ())),
                preferred_element_type=jnp.float32,
            )
            if same_position:
                row = lax.broadcasted_iota(jnp.int32, (block, TOTAL), 0)
                col = lax.broadcasted_iota(jnp.int32, (block, TOTAL), 1)
                scores = jnp.where(((row - col) & 15) == 0, scores, -1e30)
            largest = jnp.max(scores, axis=-1, keepdims=True)
            weights = jnp.exp2((scores - largest) * SCALE2).astype(jnp.bfloat16)
            summed = jnp.dot(weights, values, preferred_element_type=jnp.float32)
            done = (summed / summed[:, HD : HD + 1]).astype(jnp.bfloat16)
            ob[i * 2 : (i + 1) * 2] = done.reshape(2, 2, TOK, PAD)

    def project(st, ob, wp, ub, vb, tb, rb):
        weight = wp[...]
        theirs = ob[:, pl.ds(1 - c, 1)].reshape(TOTAL // 2, PAD)
        ub[...] = jnp.dot(theirs, weight, preferred_element_type=jnp.float32).astype(jnp.bfloat16).reshape(8, TOK, D)
        for k in FAR + (0,):
            to = chip(k, 1)
            start(remote(ub.at[to], vb.at[to], u_s.at[st, k], u_r.at[st, k], sibling))
        ours = ob[:, pl.ds(c, 1)].reshape(TOTAL // 2, PAD)
        acc[...] = jnp.dot(ours, weight, preferred_element_type=jnp.float32).reshape(8, TOK, D)
        for k in FAR:
            to = chip(k, 1)
            remote(ub.at[to], vb.at[to], u_s.at[st, k], u_r.at[st, k], sibling).wait_recv()
            tb[k] = (acc[to] + vb[to].astype(jnp.float32)).astype(jnp.bfloat16)
            start(remote(tb.at[k], rb.at[k], t_s.at[st, k], t_r.at[st, k], (frame, to * 2 + c)))
        here = chip(0, 1)
        remote(ub.at[here], vb.at[here], u_s.at[st, 0], u_r.at[st, 0], sibling).wait_recv()
        branch = acc[here] + vb[here].astype(jnp.float32)
        for k in NEAR:
            remote(tb.at[k], rb.at[k], t_s.at[st, k], t_r.at[st, k], sibling).wait_recv()
            branch = branch + rb[k].astype(jnp.float32)
        return gate_ref[st : st + 1, :] * (branch + bias_ref[st : st + 1, :])

    def finish():
        out_ref[...] = jnp.zeros_like(out_ref)
        for load in loads[2:] if len(pending) == 0 else ():
            load.wait()
        for copy in pending:
            copy.wait_send()

    loads[0].wait()
    loads[1].wait()
    latents = lat_ref[0].astype(jnp.float32)
    x0[own_rows(c), :] = normalize(latents, mod_ref[0:1, :], mod_ref[1:2, :])
    pl.semaphore_wait(barrier, len(NEAR) + 1 + 4)
    send_tokens(0, x0)
    for load in loads[2:]:
        load.wait()
    prepare(wm0, qkv0, wp0, wo0)
    gather_tokens(0, x0)
    attend(x0, wm0, o0, False)
    y0[...] = (latents + project(0, o0, wp0, u0, v0, t0, r0)).astype(jnp.bfloat16)

    for i in range(2):
        device, slot = group_place(i)
        start(remote(y0.at[i * 16 : i * 16 + 16], p0.at[slot], p_s.at[0, i], p_r.at[0, slot], device))
    prepare(wm1, qkv1, wp1, wo1)
    for i in range(2):
        remote(p0.at[i], p0.at[i], p_s.at[0, i], p_r.at[0, i], sibling).wait_recv()

    section = p0[...].reshape(TOK, D).astype(jnp.float32)
    x1[own_rows(c), :] = normalize(section, mod_ref[2:3, :], mod_ref[3:4, :])
    send_tokens(1, x1)
    gather_tokens(1, x1)
    attend(x1, wm1, o1, True)
    y1[...] = (section + project(1, o1, wp1, u1, v1, t1, r1)).astype(jnp.bfloat16)

    for i in range(2):
        device, half = frame_place(i)
        start(remote(y1.at[i * 16 : i * 16 + 16], p1.at[half], p_s.at[1, i], p_r.at[1, half], device))
    for i in range(2):
        remote(p1.at[i], p1.at[i], p_s.at[1, i], p_r.at[1, i], sibling).wait_recv()
    out_ref[...] = p1[...].reshape(1, TOK, D)
    for copy in pending:
        copy.wait_send()


def local(latents, spatial_qkv, spatial_out, temporal_qkv, temporal_out, modulation, gates, out_bias):
    bf16, f32, vmem, dma = jnp.bfloat16, jnp.float32, pltpu.VMEM, pltpu.SemaphoreType.DMA
    return pl.pallas_call(
        kernel,
        out_shape=jax.ShapeDtypeStruct(latents.shape, bf16),
        in_specs=[pl.BlockSpec(memory_space=pl.ANY)] * 8,
        out_specs=pl.BlockSpec(memory_space=pltpu.VMEM),
        scratch_shapes=[
            vmem((1, TOK, D), bf16), vmem((3, HD, D), bf16), vmem((3, HD, D), bf16),
            vmem((HD, D), bf16), vmem((HD, D), bf16),
            vmem((4, D), f32), vmem((2, D), f32), vmem((2, D), f32),
            vmem((TOTAL, D), bf16), vmem((TOTAL, D), bf16),
            vmem((3 * PAD, D), bf16), vmem((3 * PAD, D), bf16),
            vmem((PAD, D), bf16), vmem((PAD, D), bf16),
            vmem((8, 2, TOK, PAD), bf16), vmem((8, 2, TOK, PAD), bf16),
            vmem((8, TOK, D), bf16), vmem((8, TOK, D), bf16),
            vmem((8, TOK, D), bf16), vmem((8, TOK, D), bf16),
            vmem((8, TOK, D), bf16), vmem((8, TOK, D), bf16),
            vmem((8, TOK, D), bf16), vmem((8, TOK, D), bf16),
            vmem((8, TOK, D), f32),
            vmem((TOK, D), bf16), vmem((TOK, D), bf16),
            vmem((2, TOK // 2, D), bf16), vmem((2, TOK // 2, D), bf16),
            dma((8,)), dma((2, 8)), dma((2, 8)), dma((2, 8)), dma((2, 8)),
            dma((2, 8)), dma((2, 8)), dma((2, 8)), dma((2, 8)), dma((2, 2)), dma((2, 2)),
        ],
        compiler_params=pltpu.CompilerParams(
            collective_id=0, has_side_effects=True, vmem_limit_bytes=60 << 20
        ),
        name="block_pair",
    )(latents, spatial_qkv, spatial_out, temporal_qkv, temporal_out, modulation, gates, out_bias)


def solution(mesh):
    return jax.shard_map(
        local,
        mesh=mesh,
        in_specs=(
            P("frame", "head", None),
            P(None, "head", None),
            P("head", None),
            P(None, "head", None),
            P("head", None),
            P(),
            P(),
            P(),
        ),
        out_specs=P("frame", "head", None),
        check_vma=False,
    )
```

time: 108 us -> 83.9 us (0.78)
  Pallas kernels: 99.7 us -> 82.2 us
  local copies, waits for them, and re-layouts: 7.53 us -> 1.52 us
    pallas_call x1, Pallas kernels: 99.7 us -> 82.2 us  [local(): pl.pallas_call(kernel, out_shape=jax.ShapeDtypeStruct(latents.shape, bf16...]
    unnamed x17 -> x1, local copies, waits for them, and re-layouts: 7.53 us -> 1.52 us
where the time goes in v2:
time: 83.9 us; the launch traced here: 83.8 us
  Pallas kernels  82.2 us (98%)
  local copies, waits for them, and re-layouts  1.52 us (2%)
    pallas_call x1, Pallas kernels, local(): pl.pallas_call(kernel, out_shape=jax.ShapeDtypeStruct(latents.shape, bf16...  82.2 us

profile of v2, /device:TPU:1, one launch (start us, length us, event | category | flops | bytes accessed | tf_op | source)
XLA Modules:
  0.0 83.8 jit_solution(11334062236530101181)
XLA Ops:
  0.0 82.2 %block_pair.1 = bf16[1,32,1152]{2,1,0:T(8,128)(2,1)} custom-call(bf16[1,32,1152]{2,1,0:T(8,128)(2,1)} %lat_hbm.1, bf16[3,72,1152]{2,1,0:T(8,128)(2,1)} %sqkv_hbm.1, bf16[72,1152]{1,0:T(8,128)(2,1)} %so_hbm.1, bf16[3,72,1152]{2,1,0:T(8,128)(2,1)} %tqkv_hbm.1, bf16[72,1152]{1,0:T(8,128)(2,1)} %to_hbm.1, f32[4,1152]{1,0:T(4,128)} %mod_hbm.1, ...), custom_call_target="tpu_custom_call" | custom-call | tf_op jit(solution)/shard_map/block_pair/pallas_call | solution.py:213
  82.2 1.5 %copy.10 = bf16[1,32,1152]{2,1,0:T(8,128)(2,1)} copy(bf16[1,32,1152]{2,1,0:T(8,128)(2,1)} %block_pair.1) | data formatting | bytes 147456

commit v3 on v2

v3 whole, which is shorter than its diff:
```python
import jax
import jax.numpy as jnp
from jax import lax
from jax.experimental import pallas as pl
from jax.experimental.pallas import tpu as pltpu
from jax.sharding import PartitionSpec as P

HD = 72
PAD = 128
ROWS = 80
D = 1152
TOK = 32
HALF = TOK // 2
TOTAL = 512
ORDER = (0, 1, 3, 4, 2, 5, 7, 6)
SCALE2 = HD**-0.5 * 1.4426950408889634
VLIM = 60
MESH = pl.DeviceIdType.MESH


def normalize(values, shift_row, scale_row):
    centre = jnp.mean(values, axis=-1, keepdims=True)
    offsets = values - centre
    spread = jnp.mean(offsets * offsets, axis=-1, keepdims=True)
    return (offsets * lax.rsqrt(spread + 1e-6) * (1.0 + scale_row) + shift_row).astype(jnp.bfloat16)


def places():
    frame, head = lax.axis_index("frame"), lax.axis_index("head")
    return frame // 2, frame % 2, head // 8, (head // 2) % 4, head % 2


def group_place(half):
    z, yl, yh, x, c = places()
    zg = c * 8 + half * 4 + x
    turn = (z - zg + 25) % 16
    return (zg * 2 + yh, yl * 8 + ((x + turn // 4) % 4) * 2 + (turn // 2) % 2), turn % 2


def frame_place(slot):
    z, yl, yh, x, c = places()
    turn = ((x - z % 4 + 4) % 4) * 4 + c * 2 + slot
    zf = (z + turn + 7) % 16
    return (zf * 2 + yh, yl * 8 + (z % 4) * 2 + z // 8), (z // 4) % 2


def remote(src, dst, send, recv, device):
    return pltpu.make_async_remote_copy(
        src_ref=src, dst_ref=dst, send_sem=send, recv_sem=recv, device_id=device, device_id_type=MESH
    )


def kernel(
    lat_hbm, sqkv_hbm, so_hbm, tqkv_hbm, to_hbm, mod_hbm, gate_hbm, bias_hbm,
    out_ref,
    lat_ref, qkv0, qkv1, wo0, wo1, mod_ref, gate_ref, bias_ref,
    x0, x1, wm0, wm1, ws0, ws1, wr0, wr1, wp0, wp1, f0, f1, g0, g1,
    u0, u1, v0, v1, t0, t1, r0, r1, acc, y0, y1, p0,
    in_s, ag_s, ag_r, w_s, w_r, q_s, q_r, u_s, u_r, t_s, t_r, p_s, p_r,
):
    frame = lax.axis_index("frame")
    z, yl, yh, x, c = places()
    sibling = (frame, yh * 8 + x * 2 + 1 - c)
    pending = []

    loads = [
        pltpu.make_async_copy(src, dst, in_s.at[i])
        for i, (src, dst) in enumerate((
            (lat_hbm, lat_ref), (mod_hbm, mod_ref), (sqkv_hbm, qkv0), (so_hbm, wo0), (gate_hbm, gate_ref),
            (bias_hbm, bias_ref), (tqkv_hbm, qkv1), (to_hbm, wo1),
        ))
    ]
    for load in loads:
        load.start()

    def chip(i, sign):
        k = ORDER[i]
        return (frame, ((yh + k // 4) % 2) * 8 + ((x + sign * (k % 4) + 4) % 4) * 2 + c)

    def start(copy):
        copy.start()
        pending.append(copy)

    barrier = pltpu.get_barrier_semaphore()
    for i in range(2):
        pl.semaphore_signal(barrier, inc=1, device_id=group_place(i)[0], device_id_type=MESH)
        pl.semaphore_signal(barrier, inc=1, device_id=frame_place(i)[0], device_id_type=MESH)
    for i in range(7, 0, -1):
        pl.semaphore_signal(barrier, inc=1, device_id=chip(i, 1), device_id_type=MESH)
    pl.semaphore_signal(barrier, inc=1, device_id=sibling, device_id_type=MESH)

    def send_tokens(st, half, xb):
        for i in range(7, 0, -1):
            start(remote(xb.at[half, 0], xb.at[half, i], ag_s.at[st, half, i], ag_r.at[st, half, i], chip(i, 1)))

    def transpose_weights(wm, first, rows_ref):
        for m in range(3):
            rows = rows_ref[m * ROWS : (m + 1) * ROWS, :]
            rows = jnp.concatenate([rows, jnp.zeros((PAD - ROWS, D), jnp.bfloat16)], axis=0)
            wm[:, (first + m) * PAD : (first + m + 1) * PAD] = rows.T

    def prepare(st, wm, qkv_ref, ws, wr, wp, wo_ref):
        for m in range(3):
            ws[m * ROWS + 64 : (m + 1) * ROWS, :] = jnp.zeros((16, D), jnp.bfloat16)
            ws[m * ROWS : m * ROWS + HD, :] = qkv_ref[m]
        start(remote(ws, wr, w_s.at[st], w_r.at[st], sibling))
        transpose_weights(wm, 0, ws)
        wp[64:, :] = jnp.zeros((64, D), jnp.bfloat16)
        wp[:HD, :] = wo_ref[...]

    def finish_prepare(st, wm, ws, wr):
        remote(ws, wr, w_s.at[st], w_r.at[st], sibling).wait_recv()
        transpose_weights(wm, 3, wr)

    def project_tokens(st, xb, wm, fb, gb):
        for half in range(2):
            for i in range(1, 8):
                remote(
                    xb.at[half, i], xb.at[half, i], ag_s.at[st, half, i], ag_r.at[st, half, i], sibling
                ).wait_recv()
            proj = jnp.dot(xb[half].reshape(8 * HALF, D), wm[...], preferred_element_type=jnp.float32)
            lane = lax.broadcasted_iota(jnp.int32, proj.shape, 1)
            proj = jnp.where((lane == 2 * PAD + HD) | (lane == 5 * PAD + HD), 1.0, proj)
            proj = proj.astype(jnp.bfloat16).reshape(8, HALF, 6 * PAD)
            gb[half] = proj[:, :, 3 * PAD :]
            start(remote(gb.at[half], fb.at[c, half], q_s.at[st, half], q_r.at[st, half], sibling))
            fb[pl.ds(c, 1), half] = proj[:, :, : 3 * PAD].reshape(1, 8, HALF, 3 * PAD)
        for half in range(2):
            remote(gb.at[half], fb.at[1 - c, half], q_s.at[st, half], q_r.at[st, half], sibling).wait_recv()

    def attend(fb, core, half, same_position):
        keys = fb[:, :, :, :, PAD : 2 * PAD].reshape(TOTAL, PAD)
        values = fb[:, :, :, :, 2 * PAD :].reshape(TOTAL, PAD)
        block = 8 * HALF
        queries = fb[pl.ds(core, 1), half, :, :, :PAD].reshape(block, PAD)
        scores = lax.dot_general(queries, keys, (((1,), (1,)), ((), ())), preferred_element_type=jnp.float32)
        if same_position:
            row = lax.broadcasted_iota(jnp.int32, (block, TOTAL), 0)
            col = lax.broadcasted_iota(jnp.int32, (block, TOTAL), 1)
            scores = jnp.where(((row - col) & 15) == 0, scores, -1e30)
        largest = jnp.max(scores, axis=-1, keepdims=True)
        weights = jnp.exp2((scores - largest) * SCALE2).astype(jnp.bfloat16)
        summed = jnp.dot(weights, values, preferred_element_type=jnp.float32)
        return (summed / summed[:, HD : HD + 1]).astype(jnp.bfloat16)

    def attend_and_project(st, fb, wp, ub, vb, tb, rb, same_position):
        def theirs(half):
            share = jnp.dot(attend(fb, 1 - c, half, same_position), wp[...], preferred_element_type=jnp.float32)
            ub[half] = share.astype(jnp.bfloat16).reshape(8, HALF, D)
            start(remote(ub.at[half], vb.at[half], u_s.at[st, half], u_r.at[st, half], sibling))

        def ours(half):
            share = jnp.dot(attend(fb, c, half, same_position), wp[...], preferred_element_type=jnp.float32)
            acc[half] = share.reshape(8, HALF, D)

        def send_sums(half):
            remote(ub.at[half], vb.at[half], u_s.at[st, half], u_r.at[st, half], sibling).wait_recv()
            for i in range(7, 0, -1):
                tb[half, i] = (acc[half, i] + vb[half, i].astype(jnp.float32)).astype(jnp.bfloat16)
                start(remote(
                    tb.at[half, i], rb.at[half, i], t_s.at[st, half, i], t_r.at[st, half, i], chip(i, -1)
                ))

        theirs(0)
        ours(0)
        theirs(1)
        send_sums(0)
        ours(1)
        send_sums(1)

    def collect(st, half, vb, tb, rb):
        branch = acc[half, 0] + vb[half, 0].astype(jnp.float32)
        for i in range(1, 8):
            remote(
                tb.at[half, i], rb.at[half, i], t_s.at[st, half, i], t_r.at[st, half, i], sibling
            ).wait_recv()
            branch = branch + rb[half, i].astype(jnp.float32)
        return gate_ref[st : st + 1, :] * (branch + bias_ref[st : st + 1, :])

    loads[0].wait()
    loads[1].wait()
    ready = normalize(lat_ref[0].astype(jnp.float32), mod_ref[0:1, :], mod_ref[1:2, :])
    x0[0, 0] = ready[:HALF]
    x0[1, 0] = ready[HALF:]
    pl.semaphore_wait(barrier, 7 + 1 + 4)
    send_tokens(0, 0, x0)
    for load in loads[2:]:
        load.wait()
    prepare(0, wm0, qkv0, ws0, wr0, wp0, wo0)
    send_tokens(0, 1, x0)
    finish_prepare(0, wm0, ws0, wr0)
    project_tokens(0, x0, wm0, f0, g0)
    attend_and_project(0, f0, wp0, u0, v0, t0, r0, False)

    for half in range(2):
        rows = lat_ref[0, half * HALF : (half + 1) * HALF].astype(jnp.float32)
        y0[half] = (rows + collect(0, half, v0, t0, r0)).astype(jnp.bfloat16)
        device, slot = group_place(half)
        start(remote(y0.at[half], p0.at[slot], p_s.at[0, half], p_r.at[0, slot], device))
    prepare(1, wm1, qkv1, ws1, wr1, wp1, wo1)
    finish_prepare(1, wm1, ws1, wr1)

    for slot in range(2):
        remote(p0.at[slot], p0.at[slot], p_s.at[0, slot], p_r.at[0, slot], sibling).wait_recv()
        x1[slot, 0] = normalize(p0[slot].astype(jnp.float32), mod_ref[2:3, :], mod_ref[3:4, :])
        send_tokens(1, slot, x1)
    project_tokens(1, x1, wm1, f1, g1)
    attend_and_project(1, f1, wp1, u1, v1, t1, r1, True)

    for slot in range(2):
        y1[slot] = (p0[slot].astype(jnp.float32) + collect(1, slot, v1, t1, r1)).astype(jnp.bfloat16)
        device, half = frame_place(slot)
        rows = pl.ds(pl.multiple_of(half * HALF, HALF), HALF)
        start(remote(y1.at[slot], out_ref.at[0, rows], p_s.at[1, slot], p_r.at[1, half], device))
    for half in range(2):
        rows = out_ref.at[0, half * HALF : (half + 1) * HALF]
        remote(rows, rows, p_s.at[1, half], p_r.at[1, half], sibling).wait_recv()
    for copy in pending:
        copy.wait_send()


def local(latents, spatial_qkv, spatial_out, temporal_qkv, temporal_out, modulation, gates, out_bias):
    bf16, f32, vmem, dma = jnp.bfloat16, jnp.float32, pltpu.VMEM, pltpu.SemaphoreType.DMA

    def pair(*shape):
        return [vmem(shape, bf16), vmem(shape, bf16)]

    return pl.pallas_call(
        kernel,
        out_shape=jax.ShapeDtypeStruct(latents.shape, bf16),
        in_specs=[pl.BlockSpec(memory_space=pl.ANY)] * 8,
        out_specs=pl.BlockSpec(memory_space=pl.ANY),
        scratch_shapes=[
            vmem((1, TOK, D), bf16), *pair(3, HD, D), *pair(HD, D),
            vmem((4, D), f32), vmem((2, D), f32), vmem((2, D), f32),
            *pair(2, 8, HALF, D), *pair(D, 6 * PAD), *pair(3 * ROWS, D), *pair(3 * ROWS, D), *pair(PAD, D),
            *pair(2, 2, 8, HALF, 3 * PAD), *pair(2, 8, HALF, 3 * PAD),
            *pair(2, 8, HALF, D), *pair(2, 8, HALF, D), *pair(2, 8, HALF, D), *pair(2, 8, HALF, D),
            vmem((2, 8, HALF, D), f32),
            *pair(2, HALF, D), vmem((2, HALF, D), bf16),
            dma((8,)), dma((2, 2, 8)), dma((2, 2, 8)), dma((2,)), dma((2,)), dma((2, 2)), dma((2, 2)),
            dma((2, 2)), dma((2, 2)), dma((2, 2, 8)), dma((2, 2, 8)), dma((2, 2)), dma((2, 2)),
        ],
        compiler_params=pltpu.CompilerParams(
            collective_id=0, has_side_effects=True, vmem_limit_bytes=VLIM << 20
        ),
        name="block_pair",
    )(latents, spatial_qkv, spatial_out, temporal_qkv, temporal_out, modulation, gates, out_bias)


def solution(mesh):
    return jax.shard_map(
        local,
        mesh=mesh,
        in_specs=(
            P("frame", "head", None),
            P(None, "head", None),
            P("head", None),
            P(None, "head", None),
            P("head", None),
            P(),
            P(),
            P(),
        ),
        out_specs=P("frame", "head", None),
        check_vma=False,
    )
```

time: 83.9 us -> 77 us (0.918)
  Pallas kernels: 82.2 us -> 75.3 us
    pallas_call x1, Pallas kernels: 82.2 us -> 75.3 us  [local(): pl.pallas_call(kernel, out_shape=jax.ShapeDtypeStruct(latents.shape, bf16...]
where the time goes in v3:
time: 77 us; the launch traced here: 76.9 us
  Pallas kernels  75.3 us (98%)
  local copies, waits for them, and re-layouts  1.52 us (2%)
    pallas_call x1, Pallas kernels, local(): pl.pallas_call(kernel, out_shape=jax.ShapeDtypeStruct(latents.shape, bf16...  75.3 us

profile of v3, /device:TPU:1, one launch (start us, length us, event | category | flops | bytes accessed | tf_op | source)
XLA Modules:
  0.0 76.9 jit_solution(15020876399611116241)
XLA Ops:
  0.0 75.3 %block_pair.1 = bf16[1,32,1152]{2,1,0:T(8,128)(2,1)} custom-call(bf16[1,32,1152]{2,1,0:T(8,128)(2,1)} %lat_hbm.1, bf16[3,72,1152]{2,1,0:T(8,128)(2,1)} %sqkv_hbm.1, bf16[72,1152]{1,0:T(8,128)(2,1)} %so_hbm.1, bf16[3,72,1152]{2,1,0:T(8,128)(2,1)} %tqkv_hbm.1, bf16[72,1152]{1,0:T(8,128)(2,1)} %to_hbm.1, f32[4,1152]{1,0:T(4,128)} %mod_hbm.1, ...), custom_call_target="tpu_custom_call" | custom-call | tf_op jit(solution)/shard_map/block_pair/pallas_call | solution.py:228
  75.3 1.5 %copy.10 = bf16[1,32,1152]{2,1,0:T(8,128)(2,1)} copy(bf16[1,32,1152]{2,1,0:T(8,128)(2,1)} %block_pair.1) | data formatting | bytes 147456

commit v4 on v3

--- a/solution.py
+++ b/solution.py
@@ -56,7 +56,7 @@
     lat_ref, qkv0, qkv1, wo0, wo1, mod_ref, gate_ref, bias_ref,
     x0, x1, wm0, wm1, ws0, ws1, wr0, wr1, wp0, wp1, f0, f1, g0, g1,
     u0, u1, v0, v1, t0, t1, r0, r1, acc, y0, y1, p0,
-    in_s, ag_s, ag_r, w_s, w_r, q_s, q_r, u_s, u_r, t_s, t_r, p_s, p_r,
+    in_s, ag_s, ag_r, w_s, w_r, q_s, q_r, u_s, u_r, t_s, t_r, p_s, p_r, near_s,
 ):
     frame = lax.axis_index("frame")
     z, yl, yh, x, c = places()
@@ -81,13 +81,21 @@
         copy.start()
         pending.append(copy)
 
+    def signal(sem, device):
+        pl.semaphore_signal(sem, inc=1, device_id=device, device_id_type=MESH)
+
+    def signal_along_z(sem, step):
+        head = yh * 8 + x * 2 + c
+        signal(sem, (((z + step) % 16) * 2 + yl, head))
+        signal(sem, (((z + 16 - step) % 16) * 2 + yl, head))
+
     barrier = pltpu.get_barrier_semaphore()
-    for i in range(2):
-        pl.semaphore_signal(barrier, inc=1, device_id=group_place(i)[0], device_id_type=MESH)
-        pl.semaphore_signal(barrier, inc=1, device_id=frame_place(i)[0], device_id_type=MESH)
+    other_frame = (z * 2 + 1 - yl, yh * 8 + x * 2 + c)
     for i in range(7, 0, -1):
-        pl.semaphore_signal(barrier, inc=1, device_id=chip(i, 1), device_id_type=MESH)
-    pl.semaphore_signal(barrier, inc=1, device_id=sibling, device_id_type=MESH)
+        signal(barrier, chip(i, 1))
+    signal_along_z(barrier, 1)
+    signal(barrier, other_frame)
+    signal(barrier, sibling)
 
     def send_tokens(st, half, xb):
         for i in range(7, 0, -1):
@@ -112,19 +120,20 @@
         remote(ws, wr, w_s.at[st], w_r.at[st], sibling).wait_recv()
         transpose_weights(wm, 3, wr)
 
-    def project_tokens(st, xb, wm, fb, gb):
-        for half in range(2):
-            for i in range(1, 8):
-                remote(
-                    xb.at[half, i], xb.at[half, i], ag_s.at[st, half, i], ag_r.at[st, half, i], sibling
-                ).wait_recv()
-            proj = jnp.dot(xb[half].reshape(8 * HALF, D), wm[...], preferred_element_type=jnp.float32)
-            lane = lax.broadcasted_iota(jnp.int32, proj.shape, 1)
-            proj = jnp.where((lane == 2 * PAD + HD) | (lane == 5 * PAD + HD), 1.0, proj)
-            proj = proj.astype(jnp.bfloat16).reshape(8, HALF, 6 * PAD)
-            gb[half] = proj[:, :, 3 * PAD :]
-            start(remote(gb.at[half], fb.at[c, half], q_s.at[st, half], q_r.at[st, half], sibling))
-            fb[pl.ds(c, 1), half] = proj[:, :, : 3 * PAD].reshape(1, 8, HALF, 3 * PAD)
+    def project_tokens(st, half, xb, wm, fb, gb):
+        for i in range(1, 8):
+            remote(
+                xb.at[half, i], xb.at[half, i], ag_s.at[st, half, i], ag_r.at[st, half, i], sibling
+            ).wait_recv()
+        proj = jnp.dot(xb[half].reshape(8 * HALF, D), wm[...], preferred_element_type=jnp.float32)
+        lane = lax.broadcasted_iota(jnp.int32, proj.shape, 1)
+        proj = jnp.where((lane == 2 * PAD + HD) | (lane == 5 * PAD + HD), 1.0, proj)
+        proj = proj.astype(jnp.bfloat16).reshape(8, HALF, 6 * PAD)
+        gb[half] = proj[:, :, 3 * PAD :]
+        start(remote(gb.at[half], fb.at[c, half], q_s.at[st, half], q_r.at[st, half], sibling))
+        fb[pl.ds(c, 1), half] = proj[:, :, : 3 * PAD].reshape(1, 8, HALF, 3 * PAD)
+
+    def swap_tokens(st, fb, gb):
         for half in range(2):
             remote(gb.at[half], fb.at[1 - c, half], q_s.at[st, half], q_r.at[st, half], sibling).wait_recv()
 
@@ -147,6 +156,8 @@
         def theirs(half):
             share = jnp.dot(attend(fb, 1 - c, half, same_position), wp[...], preferred_element_type=jnp.float32)
             ub[half] = share.astype(jnp.bfloat16).reshape(8, HALF, D)
+            if st == 0 and half == 0:
+                pl.semaphore_wait(near_s.at[3], 1)
             start(remote(ub.at[half], vb.at[half], u_s.at[st, half], u_r.at[st, half], sibling))
 
         def ours(half):
@@ -182,14 +193,23 @@
     ready = normalize(lat_ref[0].astype(jnp.float32), mod_ref[0:1, :], mod_ref[1:2, :])
     x0[0, 0] = ready[:HALF]
     x0[1, 0] = ready[HALF:]
-    pl.semaphore_wait(barrier, 7 + 1 + 4)
+    pl.semaphore_wait(barrier, 7 + 2 + 1 + 1)
     send_tokens(0, 0, x0)
+    signal_along_z(near_s.at[0], 1)
     for load in loads[2:]:
         load.wait()
     prepare(0, wm0, qkv0, ws0, wr0, wp0, wo0)
     send_tokens(0, 1, x0)
+    pl.semaphore_wait(near_s.at[0], 2)
+    signal_along_z(near_s.at[1], 2)
     finish_prepare(0, wm0, ws0, wr0)
-    project_tokens(0, x0, wm0, f0, g0)
+    pl.semaphore_wait(near_s.at[1], 2)
+    signal_along_z(near_s.at[2], 4)
+    project_tokens(0, 0, x0, wm0, f0, g0)
+    project_tokens(0, 1, x0, wm0, f0, g0)
+    pl.semaphore_wait(near_s.at[2], 2)
+    signal(near_s.at[3], other_frame)
+    swap_tokens(0, f0, g0)
     attend_and_project(0, f0, wp0, u0, v0, t0, r0, False)
 
     for half in range(2):
@@ -204,7 +224,9 @@
         remote(p0.at[slot], p0.at[slot], p_s.at[0, slot], p_r.at[0, slot], sibling).wait_recv()
         x1[slot, 0] = normalize(p0[slot].astype(jnp.float32), mod_ref[2:3, :], mod_ref[3:4, :])
         send_tokens(1, slot, x1)
-    project_tokens(1, x1, wm1, f1, g1)
+    for half in range(2):
+        project_tokens(1, half, x1, wm1, f1, g1)
+    swap_tokens(1, f1, g1)
     attend_and_project(1, f1, wp1, u1, v1, t1, r1, True)
 
     for slot in range(2):
@@ -240,6 +262,7 @@
             *pair(2, HALF, D), vmem((2, HALF, D), bf16),
             dma((8,)), dma((2, 2, 8)), dma((2, 2, 8)), dma((2,)), dma((2,)), dma((2, 2)), dma((2, 2)),
             dma((2, 2)), dma((2, 2)), dma((2, 2, 8)), dma((2, 2, 8)), dma((2, 2)), dma((2, 2)),
+            pltpu.SemaphoreType.REGULAR((4,)),
         ],
         compiler_params=pltpu.CompilerParams(
             collective_id=0, has_side_effects=True, vmem_limit_bytes=VLIM << 20

time: 77 us -> 74.3 us (0.965)
  Pallas kernels: 75.3 us -> 72 us
    pallas_call x1, Pallas kernels: 75.3 us -> 72 us  [local(): pl.pallas_call(kernel, out_shape=jax.ShapeDtypeStruct(latents.shape, bf16...]
where the time goes in v4:
time: 74.3 us; the launch traced here: 73.5 us
  Pallas kernels  72 us (97%)
  local copies, waits for them, and re-layouts  1.52 us (2%)
    pallas_call x1, Pallas kernels, local(): pl.pallas_call(kernel, out_shape=jax.ShapeDtypeStruct(latents.shape, bf16...  72 us
    unnamed x1, local copies, waits for them, and re-layouts  1.52 us

profile of v4, /device:TPU:1, one launch (start us, length us, event | category | flops | bytes accessed | tf_op | source)
XLA Modules:
  0.0 73.5 jit_solution(4882142189212062931)
XLA Ops:
  0.0 72.0 %block_pair.1 = bf16[1,32,1152]{2,1,0:T(8,128)(2,1)} custom-call(bf16[1,32,1152]{2,1,0:T(8,128)(2,1)} %lat_hbm.1, bf16[3,72,1152]{2,1,0:T(8,128)(2,1)} %sqkv_hbm.1, bf16[72,1152]{1,0:T(8,128)(2,1)} %so_hbm.1, bf16[3,72,1152]{2,1,0:T(8,128)(2,1)} %tqkv_hbm.1, bf16[72,1152]{1,0:T(8,128)(2,1)} %to_hbm.1, f32[4,1152]{1,0:T(4,128)} %mod_hbm.1, ...), custom_call_target="tpu_custom_call" | custom-call | tf_op jit(solution)/shard_map/block_pair/pallas_call | solution.py:250
  72.0 1.5 %copy.10 = bf16[1,32,1152]{2,1,0:T(8,128)(2,1)} copy(bf16[1,32,1152]{2,1,0:T(8,128)(2,1)} %block_pair.1) | data formatting | bytes 147456

commit v5 on v4

--- a/solution.py
+++ b/solution.py
@@ -89,6 +89,11 @@
         signal(sem, (((z + step) % 16) * 2 + yl, head))
         signal(sem, (((z + 16 - step) % 16) * 2 + yl, head))
 
+    def drain(count):
+        for copy in pending[:count]:
+            copy.wait_send()
+        del pending[:count]
+
     barrier = pltpu.get_barrier_semaphore()
     other_frame = (z * 2 + 1 - yl, yh * 8 + x * 2 + c)
     for i in range(7, 0, -1):
@@ -125,13 +130,16 @@
             remote(
                 xb.at[half, i], xb.at[half, i], ag_s.at[st, half, i], ag_r.at[st, half, i], sibling
             ).wait_recv()
-        proj = jnp.dot(xb[half].reshape(8 * HALF, D), wm[...], preferred_element_type=jnp.float32)
-        lane = lax.broadcasted_iota(jnp.int32, proj.shape, 1)
-        proj = jnp.where((lane == 2 * PAD + HD) | (lane == 5 * PAD + HD), 1.0, proj)
-        proj = proj.astype(jnp.bfloat16).reshape(8, HALF, 6 * PAD)
-        gb[half] = proj[:, :, 3 * PAD :]
+        tokens = xb[half].reshape(8 * HALF, D)
+        lane = lax.broadcasted_iota(jnp.int32, (8 * HALF, 3 * PAD), 1)
+
+        def project(columns):
+            proj = jnp.dot(tokens, wm[:, columns], preferred_element_type=jnp.float32)
+            return jnp.where(lane == 2 * PAD + HD, 1.0, proj).astype(jnp.bfloat16).reshape(8, HALF, 3 * PAD)
+
+        gb[half] = project(slice(3 * PAD, 6 * PAD))
         start(remote(gb.at[half], fb.at[c, half], q_s.at[st, half], q_r.at[st, half], sibling))
-        fb[pl.ds(c, 1), half] = proj[:, :, : 3 * PAD].reshape(1, 8, HALF, 3 * PAD)
+        fb[pl.ds(c, 1), half] = project(slice(0, 3 * PAD)).reshape(1, 8, HALF, 3 * PAD)
 
     def swap_tokens(st, fb, gb):
         for half in range(2):
@@ -158,24 +166,32 @@
             ub[half] = share.astype(jnp.bfloat16).reshape(8, HALF, D)
             if st == 0 and half == 0:
                 pl.semaphore_wait(near_s.at[3], 1)
-            start(remote(ub.at[half], vb.at[half], u_s.at[st, half], u_r.at[st, half], sibling))
+            for part in (1, 0):
+                span = slice(4 * part, 4 * part + 4)
+                start(remote(
+                    ub.at[half, span], vb.at[half, span], u_s.at[st, half, part], u_r.at[st, half, part], sibling
+                ))
 
         def ours(half):
             share = jnp.dot(attend(fb, c, half, same_position), wp[...], preferred_element_type=jnp.float32)
             acc[half] = share.reshape(8, HALF, D)
 
         def send_sums(half):
-            remote(ub.at[half], vb.at[half], u_s.at[st, half], u_r.at[st, half], sibling).wait_recv()
-            for i in range(7, 0, -1):
-                tb[half, i] = (acc[half, i] + vb[half, i].astype(jnp.float32)).astype(jnp.bfloat16)
-                start(remote(
-                    tb.at[half, i], rb.at[half, i], t_s.at[st, half, i], t_r.at[st, half, i], chip(i, -1)
-                ))
+            for part in (1, 0):
+                span = slice(4 * part, 4 * part + 4)
+                remote(
+                    ub.at[half, span], vb.at[half, span], u_s.at[st, half, part], u_r.at[st, half, part], sibling
+                ).wait_recv()
+                for i in range(4 * part + 3, max(4 * part, 1) - 1, -1):
+                    tb[half, i] = (acc[half, i] + vb[half, i].astype(jnp.float32)).astype(jnp.bfloat16)
+                    start(remote(
+                        tb.at[half, i], rb.at[half, i], t_s.at[st, half, i], t_r.at[st, half, i], chip(i, -1)
+                    ))
 
         theirs(0)
         ours(0)
+        send_sums(0)
         theirs(1)
-        send_sums(0)
         ours(1)
         send_sums(1)
 
@@ -195,11 +211,11 @@
     x0[1, 0] = ready[HALF:]
     pl.semaphore_wait(barrier, 7 + 2 + 1 + 1)
     send_tokens(0, 0, x0)
+    send_tokens(0, 1, x0)
     signal_along_z(near_s.at[0], 1)
     for load in loads[2:]:
         load.wait()
     prepare(0, wm0, qkv0, ws0, wr0, wp0, wo0)
-    send_tokens(0, 1, x0)
     pl.semaphore_wait(near_s.at[0], 2)
     signal_along_z(near_s.at[1], 2)
     finish_prepare(0, wm0, ws0, wr0)
@@ -212,12 +228,14 @@
     swap_tokens(0, f0, g0)
     attend_and_project(0, f0, wp0, u0, v0, t0, r0, False)
 
+    sent = len(pending)
     for half in range(2):
         rows = lat_ref[0, half * HALF : (half + 1) * HALF].astype(jnp.float32)
         y0[half] = (rows + collect(0, half, v0, t0, r0)).astype(jnp.bfloat16)
         device, slot = group_place(half)
         start(remote(y0.at[half], p0.at[slot], p_s.at[0, half], p_r.at[0, slot], device))
     prepare(1, wm1, qkv1, ws1, wr1, wp1, wo1)
+    drain(sent)
     finish_prepare(1, wm1, ws1, wr1)
 
     for slot in range(2):
@@ -229,16 +247,17 @@
     swap_tokens(1, f1, g1)
     attend_and_project(1, f1, wp1, u1, v1, t1, r1, True)
 
+    sent = len(pending)
     for slot in range(2):
         y1[slot] = (p0[slot].astype(jnp.float32) + collect(1, slot, v1, t1, r1)).astype(jnp.bfloat16)
         device, half = frame_place(slot)
         rows = pl.ds(pl.multiple_of(half * HALF, HALF), HALF)
         start(remote(y1.at[slot], out_ref.at[0, rows], p_s.at[1, slot], p_r.at[1, half], device))
+    drain(sent)
     for half in range(2):
         rows = out_ref.at[0, half * HALF : (half + 1) * HALF]
         remote(rows, rows, p_s.at[1, half], p_r.at[1, half], sibling).wait_recv()
-    for copy in pending:
-        copy.wait_send()
+    drain(len(pending))
 
 
 def local(latents, spatial_qkv, spatial_out, temporal_qkv, temporal_out, modulation, gates, out_bias):
@@ -261,7 +280,7 @@
             vmem((2, 8, HALF, D), f32),
             *pair(2, HALF, D), vmem((2, HALF, D), bf16),
             dma((8,)), dma((2, 2, 8)), dma((2, 2, 8)), dma((2,)), dma((2,)), dma((2, 2)), dma((2, 2)),
-            dma((2, 2)), dma((2, 2)), dma((2, 2, 8)), dma((2, 2, 8)), dma((2, 2)), dma((2, 2)),
+            dma((2, 2, 2)), dma((2, 2, 2)), dma((2, 2, 8)), dma((2, 2, 8)), dma((2, 2)), dma((2, 2)),
             pltpu.SemaphoreType.REGULAR((4,)),
         ],
         compiler_params=pltpu.CompilerParams(

time: 74.3 us -> 73.2 us (0.985)
  no operation moved by 1% of the time
where the time goes in v5:
time: 73.2 us; the launch traced here: 72.9 us
  Pallas kernels  71.4 us (98%)
  local copies, waits for them, and re-layouts  1.52 us (2%)
    pallas_call x1, Pallas kernels, local(): pl.pallas_call(kernel, out_shape=jax.ShapeDtypeStruct(latents.shape, bf16...  71.4 us
    unnamed x1, local copies, waits for them, and re-layouts  1.52 us

profile of v5, /device:TPU:1, one launch (start us, length us, event | category | flops | bytes accessed | tf_op | source)
XLA Modules:
  0.0 72.9 jit_solution(9372887345631318420)
XLA Ops:
  0.0 71.4 %block_pair.1 = bf16[1,32,1152]{2,1,0:T(8,128)(2,1)} custom-call(bf16[1,32,1152]{2,1,0:T(8,128)(2,1)} %lat_hbm.1, bf16[3,72,1152]{2,1,0:T(8,128)(2,1)} %sqkv_hbm.1, bf16[72,1152]{1,0:T(8,128)(2,1)} %so_hbm.1, bf16[3,72,1152]{2,1,0:T(8,128)(2,1)} %tqkv_hbm.1, bf16[72,1152]{1,0:T(8,128)(2,1)} %to_hbm.1, f32[4,1152]{1,0:T(4,128)} %mod_hbm.1, ...), custom_call_target="tpu_custom_call" | custom-call | tf_op jit(solution)/shard_map/block_pair/pallas_call | solution.py:269
  71.4 1.5 %copy.10 = bf16[1,32,1152]{2,1,0:T(8,128)(2,1)} copy(bf16[1,32,1152]{2,1,0:T(8,128)(2,1)} %block_pair.1) | data formatting | bytes 147456

commit v6 on v5

--- a/solution.py
+++ b/solution.py
@@ -70,7 +70,7 @@
             (bias_hbm, bias_ref), (tqkv_hbm, qkv1), (to_hbm, wo1),
         ))
     ]
-    for load in loads:
+    for load in loads[:2]:
         load.start()
 
     def chip(i, sign):
@@ -101,6 +101,8 @@
     signal_along_z(barrier, 1)
     signal(barrier, other_frame)
     signal(barrier, sibling)
+    for load in loads[2:]:
+        load.start()
 
     def send_tokens(st, half, xb):
         for i in range(7, 0, -1):

time: 73.2 us -> 73.3 us (level)
  no operation moved by 1% of the time
where the time goes in v6:
time: 73.3 us; the launch traced here: 72.8 us
  Pallas kernels  71.2 us (97%)
  local copies, waits for them, and re-layouts  1.52 us (2%)
    pallas_call x1, Pallas kernels, local(): pl.pallas_call(kernel, out_shape=jax.ShapeDtypeStruct(latents.shape, bf16...  71.2 us
    unnamed x1, local copies, waits for them, and re-layouts  1.52 us

profile of v6, /device:TPU:1, one launch (start us, length us, event | category | flops | bytes accessed | tf_op | source)
XLA Modules:
  0.0 72.8 jit_solution(4931547414287703168)
XLA Ops:
  0.0 71.2 %block_pair.1 = bf16[1,32,1152]{2,1,0:T(8,128)(2,1)} custom-call(bf16[1,32,1152]{2,1,0:T(8,128)(2,1)} %lat_hbm.1, bf16[3,72,1152]{2,1,0:T(8,128)(2,1)} %sqkv_hbm.1, bf16[72,1152]{1,0:T(8,128)(2,1)} %so_hbm.1, bf16[3,72,1152]{2,1,0:T(8,128)(2,1)} %tqkv_hbm.1, bf16[72,1152]{1,0:T(8,128)(2,1)} %to_hbm.1, f32[4,1152]{1,0:T(4,128)} %mod_hbm.1, ...), custom_call_target="tpu_custom_call" | custom-call | tf_op jit(solution)/shard_map/block_pair/pallas_call | solution.py:271
  71.2 1.5 %copy.10 = bf16[1,32,1152]{2,1,0:T(8,128)(2,1)} copy(bf16[1,32,1152]{2,1,0:T(8,128)(2,1)} %block_pair.1) | data formatting | bytes 147456
